TPU v7x, 32 devices: a whole 2x2x4 slice. The times are simulated.
32 devices in a mesh: cp: 8 (over z, x), grp: 4 (over y, core).
Axes of the slice: x: 2, y: 2, z: 4, core: 2. Of those that a mesh axis runs over, the one named last changes fastest.
Arguments:
- queries: bfloat16 [8192, 8192], P(('cp', 'grp')), may hold values from -60 to 60
- keys: bfloat16 [8192, 1024], P(('cp', 'grp')), may hold values from -4 to 4
- values: bfloat16 [8192, 1024], P(('cp', 'grp')), may hold values from -6 to 6
- doc_lengths: int32 [8, 3], P('cp'), may hold values from 1 to 768, 1024 in all within a row
- send_tile: int32 [32, 16], P(('cp', 'grp')), may hold values from 0 to 8, as said below
- take_slot: int32 [32, 8], P(('cp', 'grp')), may hold values from 0 to 15, as said below
Outputs:
- attended: bfloat16 [8192, 8192], P(('cp', 'grp'))
Inputs may be any that keep to these rules, and one draw needn't show every extreme that they name: `send_tile`: entry c2 * 2 + s of row d = c * 4 + g names the arrival tile (0 to 7) that device (c, g) sends in slot s to device (c2, g), and 8 marks an empty slot. Every tile of a device is sent exactly once; each device sends 2 tiles to each of exactly 4 peers and none to the others. `take_slot`: row d2 lists, for each owner tile of device d2, the received slot c * 2 + s (slot s of the tiles sent by device (c, g) of the same g) that fills it; every filled send slot fills exactly one owner tile, so each device receives from exactly 4 peers.
All inputs are finite; a program needn't handle non-finite values.
Results may differ from a plain program's by a relative error of at most 0.0037.
Values may be sent and summed in bfloat16 or wider, within the bound.
A program may use at most 128 MiB of HBM per device.

v0:
```python
import math

import jax
import jax.numpy as jnp
from jax import lax
from jax.sharding import PartitionSpec as P

QUERY_HEADS = 64
KEY_VALUE_HEADS = 8
HEAD_SIZE = 128


def local(queries, keys, values, doc_lengths, send_tile, take_slot):
    tok_rows = queries.shape[0]
    peer_count = lax.axis_size("cp")
    member_count = lax.axis_size("grp")
    tile_rows = tok_rows // peer_count
    slot_count = send_tile.shape[1] // peer_count
    chosen = send_tile[0]
    placed = take_slot[0]

    def outgoing(source):
        tiled = source.reshape(peer_count, tile_rows, source.shape[1])
        picked = jnp.take(tiled, chosen, axis=0, mode="fill", fill_value=0)
        return picked.reshape(peer_count * slot_count * tile_rows, source.shape[1])

    def incoming(source):
        tiled = source.reshape(peer_count * slot_count, tile_rows, source.shape[1])
        return jnp.take(tiled, placed, axis=0).reshape(tok_rows, source.shape[1])

    got_queries, got_keys, got_values = (
        lax.all_to_all(outgoing(queries), "cp", split_axis=0, concat_axis=0, tiled=True),
        lax.all_to_all(outgoing(keys), "cp", split_axis=0, concat_axis=0, tiled=True),
        lax.all_to_all(outgoing(values), "cp", split_axis=0, concat_axis=0, tiled=True),
    )
    own_queries = incoming(got_queries)
    all_keys, all_values = (
        lax.all_gather(incoming(got_keys), "grp", axis=0, tiled=True),
        lax.all_gather(incoming(got_values), "grp", axis=0, tiled=True),
    )
    member = lax.axis_index("grp")
    group_length = member_count * tok_rows
    doc_ends = jnp.cumsum(doc_lengths[0])
    positions = jnp.arange(group_length, dtype=jnp.int32)
    doc_all = jnp.sum((positions[:, None] >= doc_ends[None, :]).astype(jnp.int32), axis=1)
    query_pos = member * tok_rows + jnp.arange(tok_rows, dtype=jnp.int32)
    doc_query = lax.dynamic_slice_in_dim(doc_all, member * tok_rows, tok_rows)
    allowed = (doc_query[:, None] == doc_all[None, :]) & (positions[None, :] <= query_pos[:, None])
    queries_per_group = QUERY_HEADS // KEY_VALUE_HEADS
    head_width = queries_per_group * HEAD_SIZE
    score_scale = 1.0 / math.sqrt(HEAD_SIZE)

    def single_head_output(head_number_index, result):
        query_head = lax.dynamic_slice_in_dim(
            own_queries, head_number_index * head_width, head_width, 1
        )
        query_head = query_head.reshape(tok_rows, queries_per_group, HEAD_SIZE)
        key_head = lax.dynamic_slice_in_dim(all_keys, head_number_index * HEAD_SIZE, HEAD_SIZE, 1)
        value_head = lax.dynamic_slice_in_dim(
            all_values, head_number_index * HEAD_SIZE, HEAD_SIZE, 1
        )
        scores = (
            jnp.einsum("qgd,kd->gqk", query_head, key_head, preferred_element_type=jnp.float32)
            * score_scale
        )
        scores = jnp.where(allowed[None], scores, -jnp.inf)
        row_max = jnp.max(scores, axis=2, keepdims=True)
        weights = jnp.exp(scores - row_max)
        totals = jnp.sum(weights, axis=2)
        rounded = weights.astype(jnp.bfloat16)
        summed = jnp.einsum("gqk,kd->qgd", rounded, value_head, preferred_element_type=jnp.float32)
        mixed = (summed / jnp.transpose(totals)[:, :, None]).astype(jnp.bfloat16)
        return lax.dynamic_update_slice_in_dim(
            result, mixed.reshape(tok_rows, head_width), head_number_index * head_width, 1
        )

    starting_state = jnp.zeros((tok_rows, QUERY_HEADS * HEAD_SIZE), jnp.bfloat16)
    return lax.fori_loop(0, KEY_VALUE_HEADS, single_head_output, starting_state)


def solution(mesh):
    return jax.shard_map(
        local,
        mesh=mesh,
        in_specs=(
            P(("cp", "grp"), None),
            P(("cp", "grp"), None),
            P(("cp", "grp"), None),
            P("cp", None),
            P(("cp", "grp"), None),
            P(("cp", "grp"), None),
        ),
        out_specs=P(("cp", "grp"), None),
        check_vma=False,
    )
```

profile of v0, /device:TPU:0, one launch (start us, length us, event | category | flops | bytes accessed | tf_op | source)
XLA Modules:
  0.0 359.9 jit_solution(1103790393218674370)
XLA Ops:
  6.5 0.7 compare_select_fusion.2
  7.3 0.7 compare_and_fusion.2
  7.9 0.6 gather_fusion.2
  8.6 1.7 gather_fusion.4
  10.2 1.5 broadcast_select_fusion
  11.8 7.3 %all-to-all-start = ((bf16[8,64,1024]{2,1,0:T(8,128)(2,1)}), bf16[8,64,1024]{2,1,0:T(8,128)(2,1)S(1)}, u32[]{:S(2)}, u32[]{:S(2)}) async-start(bf16[8,64,1024]{2,1,0:T(8,128)(2,1)} %bitcast.88), calls=%async_computation | async-start | bytes 2097152 | tf_op jit(solution)/shard_map/all_to_all | solution.py:34
  19.0 0.6 broadcast.188
  19.6 0.6 reduce.3
  20.5 6.9 %gather_fusion = bf16[16,32,8192]{2,1,0:T(8,128)(2,1)} fusion(bf16[8,32,8192]{2,1,0:T(8,128)(2,1)} %bitcast.86, s32[1024]{0:T(1024)S(1)} %pad_clamp_fusion.1), kind=kCustom, calls=%fused_computation.4 | custom fusion | bytes 16777280 | tf_op jit(solution)/shard_map/jit(_take)/gather | solution.py:24
  27.4 17.4 %all-to-all-done = bf16[8,64,1024]{2,1,0:T(8,128)(2,1)S(1)} async-done(((bf16[8,64,1024]{2,1,0:T(8,128)(2,1)}), bf16[8,64,1024]{2,1,0:T(8,128)(2,1)S(1)}, u32[]{:S(2)}, u32[]{:S(2)}) %all-to-all-start) | async-done | bytes 1048608 | tf_op jit(solution)/shard_map/all_to_all | solution.py:34
  44.8 3.6 all-to-all-start.1
  48.4 7.2 %bitcast_select_fusion.1 = bf16[8,64,8192]{2,1,0:T(8,128)(2,1)} fusion(pred[8,64]{1,0:T(8,128)(4,1)S(1)} %broadcast_in_dim.93, bf16[8,64,8192]{2,1,0:T(8,128)(2,1)} %bitcast.85), kind=kLoop, calls=%fused_computation.29 | loop fusion | flops 4194304 | bytes 16777728 | tf_op jit(solution)/shard_map/jit(_take)/select_n | solution.py:24
  55.6 18.7 %all-to-all-done.1 = bf16[8,64,1024]{2,1,0:T(8,128)(2,1)S(1)} async-done(((bf16[8,64,1024]{2,1,0:T(8,128)(2,1)}), bf16[8,64,1024]{2,1,0:T(8,128)(2,1)S(1)}, u32[]{:S(2)}, u32[]{:S(2)}) %all-to-all-start.1) | async-done | bytes 1048608 | tf_op jit(solution)/shard_map/all_to_all | solution.py:33
  74.3 5.0 %all-to-all-start.2 = ((bf16[8,64,8192]{2,1,0:T(8,128)(2,1)}), bf16[8,64,8192]{2,1,0:T(8,128)(2,1)}, u32[]{:S(2)}, u32[]{:S(2)}) async-start(bf16[8,64,8192]{2,1,0:T(8,128)(2,1)} %bitcast_select_fusion.1), calls=%async_computation.2 | async-start | bytes 16777216 | tf_op jit(solution)/shard_map/all_to_all | solution.py:32
  79.4 0.6 gather_fusion.3
  80.0 0.6 gather_fusion.5
  80.6 1.1 broadcast_select_fusion.2
  81.8 0.7 all-gather.5.cloned.1.call-update
  83.1 178.7 %all-to-all-done.2 = bf16[8,64,8192]{2,1,0:T(8,128)(2,1)} async-done(((bf16[8,64,8192]{2,1,0:T(8,128)(2,1)}), bf16[8,64,8192]{2,1,0:T(8,128)(2,1)}, u32[]{:S(2)}, u32[]{:S(2)}) %all-to-all-start.2) | async-done | bytes 8388640 | tf_op jit(solution)/shard_map/all_to_all | solution.py:32
  261.7 6.2 %gather_fusion.1 = bf16[8,32,8192]{2,1,0:T(8,128)(2,1)} fusion(bf16[16,32,8192]{2,1,0:T(8,128)(2,1)} %bitcast.14, s32[1024]{0:T(1024)S(1)} %pad_clamp_fusion), kind=kCustom, calls=%fused_computation.5 | custom fusion | bytes 8388640 | tf_op jit(solution)/shard_map/jit(_take)/gather | solution.py:29
  267.9 4.6 %bitcast_select_fusion.2 = bf16[256,8192]{1,0:T(8,128)(2,1)} fusion(bf16[8,32,8192]{2,1,0:T(8,128)(2,1)} %gather_fusion.1, pred[256]{0:T(512)(128)(4,1)S(1)} %broadcast_in_dim.90), kind=kLoop, calls=%fused_computation.30 | loop fusion | flops 2097152 | bytes 8388864 | tf_op jit(solution)/shard_map/jit(_take)/select_n | solution.py:29
  272.5 2.5 broadcast_in_dim.88.clone
  275.0 78.0 %while.14 = (s32[]{:T(128)}, bf16[256,8192]{1,0:T(8,128)(2,1)}, bf16[1024,1024]{1,0:T(8,128)(2,1)}, bf16[1024,1024]{1,0:T(8,128)(2,1)}, bf16[256,8192]{1,0:T(8,1...) while((s32[]{:T(128)}, bf16[256,8192]{1,0:T(8,128)(2,1)}, ...), condition=%wide.region_5.8_spmd.clone, body=%wide.region_2.0_spmd.clone.sunk | while | flops 1098117120 | bytes 32028904 | solution.py:78
  275.0 1.1 constant_dynamic-slice_fusion.2
  276.3 0.3 fusion.35
  276.6 2.3 fusion.36
  278.9 1.7 fusion.37
  280.6 3.1 divide_convert_fusion.2
  283.9 0.8 constant_dynamic-update-slice_fusion.2
  284.8 1.1 constant_dynamic-slice_fusion.2
  286.3 2.3 fusion.36
  288.6 1.7 fusion.37
  290.3 3.1 divide_convert_fusion.2
  293.7 0.8 constant_dynamic-update-slice_fusion.2
  294.5 1.1 constant_dynamic-slice_fusion.2
  296.1 2.3 fusion.36
  298.4 1.7 fusion.37
  300.1 3.1 divide_convert_fusion.2
  303.4 0.8 constant_dynamic-update-slice_fusion.2
  304.3 1.1 constant_dynamic-slice_fusion.2
  305.8 2.3 fusion.36
  308.1 1.7 fusion.37
  309.8 3.1 divide_convert_fusion.2
  313.2 0.8 constant_dynamic-update-slice_fusion.2
  314.0 1.1 constant_dynamic-slice_fusion.2
  315.6 2.3 fusion.36
  317.9 1.7 fusion.37
  319.6 3.1 divide_convert_fusion.2
  322.9 0.8 constant_dynamic-update-slice_fusion.2
  323.8 1.1 constant_dynamic-slice_fusion.2
  325.3 2.3 fusion.36
  327.6 1.7 fusion.37
  329.3 3.1 divide_convert_fusion.2
  332.7 0.8 constant_dynamic-update-slice_fusion.2
  333.5 1.1 constant_dynamic-slice_fusion.2
  335.1 2.3 fusion.36
  337.4 1.7 fusion.37
  339.1 3.1 divide_convert_fusion.2
  342.5 0.8 constant_dynamic-update-slice_fusion.2
  343.3 1.1 constant_dynamic-slice_fusion.2
  344.8 2.3 fusion.36
  347.1 1.7 fusion.37
  348.8 3.1 divide_convert_fusion.2
  352.2 0.8 constant_dynamic-update-slice_fusion.2
  (54 shorter events, 6.0 us)
Async XLA Ops:
  6.5 1.4 copy-start
  6.5 13.1 %copy-start.1 = (s32[1,16]{1,0:T(1,128)S(1)}, s32[1,16]{1,0:T(1,128)}, u32[]{:S(2)}) copy-start(s32[1,16]{1,0:T(1,128)} %param.16) | copy-start | bytes 196
  11.8 33.0 %all-to-all-start = ((bf16[8,64,1024]{2,1,0:T(8,128)(2,1)}), bf16[8,64,1024]{2,1,0:T(8,128)(2,1)S(1)}, u32[]{:S(2)}, u32[]{:S(2)}) async-start(bf16[8,64,1024]{2,1,0:T(8,128)(2,1)} %bitcast.88), calls=%async_computation | async-start | bytes 2097152 | tf_op jit(solution)/shard_map/all_to_all | solution.py:34
  44.8 29.5 %all-to-all-start.1 = ((bf16[8,64,1024]{2,1,0:T(8,128)(2,1)}), bf16[8,64,1024]{2,1,0:T(8,128)(2,1)S(1)}, u32[]{:S(2)}, u32[]{:S(2)}) async-start(bf16[8,64,1024]{2,1,0:T(8,128)(2,1)} %bitcast.7), calls=%async_computation.1 | async-start | bytes 2097152 | tf_op jit(solution)/shard_map/all_to_all | solution.py:33
  55.6 23.8 %copy-start.3 = (s32[1,8]{1,0:T(1,128)S(1)}, s32[1,8]{1,0:T(1,128)}, u32[]{:S(2)}) copy-start(s32[1,8]{1,0:T(1,128)} %param.17) | copy-start | bytes 100
  55.6 26.9 %copy-start.2 = (s32[1,3]{1,0:T(1,128)S(1)}, s32[1,3]{1,0:T(1,128)}, u32[]{:S(2)}) copy-start(s32[1,3]{1,0:T(1,128)} %param.15) | copy-start | bytes 40
  74.3 187.4 %all-to-all-start.2 = ((bf16[8,64,8192]{2,1,0:T(8,128)(2,1)}), bf16[8,64,8192]{2,1,0:T(8,128)(2,1)}, u32[]{:S(2)}, u32[]{:S(2)}) async-start(bf16[8,64,8192]{2,1,0:T(8,128)(2,1)} %bitcast_select_fusion.1), calls=%async_computation.2 | async-start | bytes 16777216 | tf_op jit(solution)/shard_map/all_to_all | solution.py:32
  79.3 193.2 %all-gather.3.cloned.1.call-start = ((), (), s32[]{:S(2)}) async-start(), calls=%async_computation.3 | async-start | bytes 2621440 | tf_op jit(solution)/shard_map/all_gather | solution.py:39
  81.8 190.8 %all-gather.5.cloned.1.call-start = ((), (), s32[]{:S(2)}) async-start(), calls=%async_computation.4 | async-start | bytes 2621440 | tf_op jit(solution)/shard_map/all_gather | solution.py:38
Sparse Core Ops, SparseCore 0:
  81.9 23.8 all-gather.2
  107.4 22.5 all-gather.4
where the time goes:
time: 361 us; the launch traced here: 360 us
  waiting for transfers between devices  215 us (60%)
  matrix products  43.4 us (12%)
  local copies, waits for them, and re-layouts  38.7 us (11%)
  other arithmetic  32.5 us (9%)
  starting transfers between devices  15.9 us (4%)
  between operations  13.5 us (4%)
    all_to_all x1, waiting for transfers between devices, local(): lax.all_to_all(outgoing(queries), 'cp', split_axis=0, concat_axis=0, tile...  179 us
    dot_general x8, matrix products, single_head_output(): jnp.einsum('gqk,kd->qgd', rounded, value_head, preferred_element_type=jnp...  25.1 us
    all_to_all x1, waiting for transfers between devices, local(): lax.all_to_all(outgoing(keys), 'cp', split_axis=0, concat_axis=0, tiled=T...  18.7 us
    dot_general x8, matrix products, single_head_output(): jnp.einsum('qgd,kd->gqk', query_head, key_head, preferred_element_type=jn...  18.3 us
    all_to_all x1, waiting for transfers between devices, local(): lax.all_to_all(outgoing(values), 'cp', split_axis=0, concat_axis=0, tiled...  17.4 us
    reduce_sum x8, other arithmetic, single_head_output(): totals = jnp.sum(weights, axis=2)  13.6 us
    dynamic_slice x16, local copies, waits for them, and re-layouts, single_head_output(): lax.dynamic_slice_in_dim(own_queries, head_number_index * head_width, hea...  10.2 us
    select_n x4, other arithmetic, outgoing(): picked = jnp.take(tiled, chosen, axis=0, mode='fill', fill_value=0)  9.49 us
  transfers between devices with their start and end apart: 5, of which 3 were waited for; matrix products, arithmetic and copies ran while one was open for 8% of the time, Pallas kernels for 0%

commit v1 on v0

v1 whole, which is shorter than its diff:
```python
import functools
import math

import jax
import jax.numpy as jnp
from jax import lax
from jax.experimental import pallas as pl
from jax.experimental.pallas import tpu as pltpu
from jax.sharding import PartitionSpec as P

QUERY_HEADS = 64
KEY_VALUE_HEADS = 8
HEAD_SIZE = 128
PER_GROUP = QUERY_HEADS // KEY_VALUE_HEADS
HEAD_WIDTH = PER_GROUP * HEAD_SIZE
CHUNKS = 4


def pack_kernel(chosen_ref, *refs, tiles, slots, spans):
    count = len(spans)
    sources, targets, sems = refs[: len(refs) - 1 - count], refs[-1 - count : -1], refs[-1]

    def each(act):
        def one(slot, carry):
            tile = chosen_ref[slot]

            @pl.when(tile < tiles)
            def _():
                for number, (source, start, width) in enumerate(spans):
                    piece = sources[source].at[tile, :, pl.ds(start, width)]
                    act(pltpu.make_async_copy(piece, targets[number].at[slot], sems.at[number, slot]))

            return carry

        lax.fori_loop(0, slots, one, 0)

    each(lambda copy: copy.start())
    each(lambda copy: copy.wait())


def pack(chosen, arrays, spans, tile_rows):
    tiles, slots = arrays[0].shape[0] // tile_rows, chosen.shape[0]
    tiled = [a.reshape(tiles, tile_rows, a.shape[1]) for a in arrays]
    any_spec = pl.BlockSpec(memory_space=pl.ANY)
    return pl.pallas_call(
        functools.partial(pack_kernel, tiles=tiles, slots=slots, spans=spans),
        out_shape=[jax.ShapeDtypeStruct((slots, tile_rows, w), jnp.bfloat16) for _, _, w in spans],
        grid_spec=pltpu.PrefetchScalarGridSpec(
            num_scalar_prefetch=1,
            grid=(1,),
            in_specs=[any_spec] * len(tiled),
            out_specs=[any_spec] * len(spans),
            scratch_shapes=[pltpu.SemaphoreType.DMA((len(spans), slots))],
        ),
    )(chosen, *tiled)


def attend_kernel(take_ref, lengths_ref, info_ref, *refs, tiles, docs):
    pieces = refs[:tiles]
    key_ref, value_ref = refs[tiles : tiles + 2]
    out_ref, bias_ref = refs[-2], refs[-1]
    rows, length = bias_ref.shape

    @pl.when(pl.program_id(0) == 0)
    def _():
        spot = info_ref[0] + lax.broadcasted_iota(jnp.int32, (rows, 1), 0)
        begin = jnp.zeros((rows, 1), jnp.int32)
        end = 0
        for k in range(docs):
            end = end + lengths_ref[k]
            begin = jnp.where(spot >= end, end, begin)
        column = lax.broadcasted_iota(jnp.int32, (rows, length), 1)
        bias_ref[...] = jnp.where((column >= begin) & (column <= spot), 0.0, -jnp.inf)

    keys, values = key_ref[...], value_ref[...]
    factor = math.log2(math.e) / math.sqrt(HEAD_SIZE)
    for head in range(PER_GROUP):
        span = slice(head * HEAD_SIZE, (head + 1) * HEAD_SIZE)
        query = jnp.concatenate([p[0, :, span] for p in pieces], axis=0)
        scores = lax.dot_general(
            query, keys, (((1,), (1,)), ((), ())), preferred_element_type=jnp.float32
        )
        scores = scores + bias_ref[...]
        top = jnp.max(scores, axis=1, keepdims=True)
        weights = jnp.exp2((scores - top) * factor)
        totals = jnp.sum(weights, axis=1, keepdims=True)
        summed = jnp.dot(weights.astype(jnp.bfloat16), values, preferred_element_type=jnp.float32)
        out_ref[:, span] = (summed / totals).astype(jnp.bfloat16)


def attend(take, lengths, info, got, keys, values, result, first):
    tiles, (_, tile_rows, width) = take.shape[0], got.shape
    rows, length = tiles * tile_rows, keys.shape[0]
    heads = width // HEAD_WIDTH
    in_specs = [
        pl.BlockSpec((1, tile_rows, HEAD_WIDTH), lambda h, t, e, n, i=i: (t[i], 0, h))
        for i in range(tiles)
    ]
    in_specs += [pl.BlockSpec((length, HEAD_SIZE), lambda h, t, e, n: (0, first + h))] * 2
    operands = [got] * tiles + [keys, values]
    aliases = {}
    if result is not None:
        in_specs.append(pl.BlockSpec(memory_space=pl.ANY))
        aliases = {3 + len(operands): 0}
        operands.append(result)
    pairs = heads * PER_GROUP * rows * length
    return pl.pallas_call(
        functools.partial(attend_kernel, tiles=tiles, docs=lengths.shape[0]),
        out_shape=jax.ShapeDtypeStruct((rows, QUERY_HEADS * HEAD_SIZE), jnp.bfloat16),
        grid_spec=pltpu.PrefetchScalarGridSpec(
            num_scalar_prefetch=3,
            grid=(heads,),
            in_specs=in_specs,
            out_specs=pl.BlockSpec((rows, HEAD_WIDTH), lambda h, t, e, n: (0, first + h)),
            scratch_shapes=[pltpu.VMEM((rows, length), jnp.float32)],
        ),
        input_output_aliases=aliases,
        compiler_params=pltpu.CompilerParams(vmem_limit_bytes=40 * 2**20),
        cost_estimate=pl.CostEstimate(
            flops=4 * pairs * HEAD_SIZE, bytes_accessed=2 * rows * width * 2, transcendentals=pairs
        ),
    )(take, lengths, info, *operands)


def local(queries, keys, values, doc_lengths, send_tile, take_slot):
    tok_rows = queries.shape[0]
    peer_count = lax.axis_size("cp")
    tile_rows = tok_rows // peer_count
    chosen, placed = send_tile[0], take_slot[0]
    kv_width = KEY_VALUE_HEADS * HEAD_SIZE
    q_width = QUERY_HEADS * HEAD_SIZE // CHUNKS
    spans = [(1, 0, kv_width), (2, 0, kv_width)]
    spans += [(0, i * q_width, q_width) for i in range(CHUNKS)]
    sent = pack(chosen, [queries, keys, values], spans, tile_rows)

    def exchange(source):
        return lax.all_to_all(source, "cp", split_axis=0, concat_axis=0, tiled=True)

    def share(source):
        got = exchange(source).reshape(-1, kv_width)
        (own,) = pack(placed, [got], [(0, 0, kv_width)], tile_rows)
        return lax.all_gather(own.reshape(tok_rows, kv_width), "grp", axis=0, tiled=True)

    all_keys, all_values = share(sent[0]), share(sent[1])
    lengths = doc_lengths[0]
    info = (lax.axis_index("grp") * tok_rows).astype(jnp.int32).reshape(1)
    result = None
    for i in range(CHUNKS):
        got = exchange(sent[2 + i])
        first = i * (KEY_VALUE_HEADS // CHUNKS)
        result = attend(placed, lengths, info, got, all_keys, all_values, result, first)
    return result


def solution(mesh):
    both = P(("cp", "grp"), None)
    return jax.shard_map(
        local,
        mesh=mesh,
        in_specs=(both, both, both, P("cp", None), both, both),
        out_specs=both,
        check_vma=False,
    )
```

time: 361 us -> 460 us (1.27)
  Pallas kernels: 0 us -> 240 us
  waiting for transfers between devices: 215 us -> 25.8 us
  blocking collectives: 0 us -> 165 us
  matrix products: 43.4 us -> 0 us
  other arithmetic: 32.5 us -> 0 us
  local copies, waits for them, and re-layouts: 38.7 us -> 6.39 us
  starting transfers between devices: 15.9 us -> 8.96 us
    pallas_call x0 -> x7, Pallas kernels: none -> 240 us  [the longest x3 197 us: pack(): pl.pallas_call(functools.partial(pack_kernel, tiles=tiles, slots=slots, s...]
    all_to_all x3 -> x2, waiting for transfers between devices: 215 us -> 11.6 us  [exchange(): return lax.all_to_all(source, 'cp', split_axis=0, concat_axis=0, tiled=True)]
    all_to_all x0 -> x4, blocking collectives: none -> 165 us  [exchange(): return lax.all_to_all(source, 'cp', split_axis=0, concat_axis=0, tiled=True)]
    dot_general x16 -> x0, matrix products: 43.4 us -> none  [the longest x8 25.1 us: single_head_output(): jnp.einsum('gqk,kd->qgd', rounded, value_head, preferred_element_type=jnp...]
    gather x6 -> x0, local copies, waits for them, and re-layouts: 16.5 us -> none  [the longest x3 9.18 us: outgoing(): picked = jnp.take(tiled, chosen, axis=0, mode='fill', fill_value=0)]
    select_n x8 -> x0, other arithmetic: 15.2 us -> none  [the longest x4 9.49 us: outgoing(): picked = jnp.take(tiled, chosen, axis=0, mode='fill', fill_value=0)]
    all_gather x2, waiting for transfers between devices: 0.01 us -> 14.2 us  [share(): lax.all_gather(own.reshape(tok_rows, kv_width), 'grp', axis=0, tiled=True)]
    reduce_sum x9 -> x0, other arithmetic: 13.7 us -> none  [the longest x8 13.6 us: single_head_output(): totals = jnp.sum(weights, axis=2)]
  transfers between devices with their start and end apart: 5 -> 4, of which waited for: 3 -> 2; matrix products, arithmetic and copies ran while one was open for 8% -> 0% of each run, Pallas kernels for 0% -> 15%
where the time goes in v1:
time: 460 us
  Pallas kernels  240 us (52%)
  blocking collectives  165 us (36%)
  waiting for transfers between devices  25.8 us (6%)
  between operations  13.5 us (3%)
  starting transfers between devices  8.96 us (2%)
  local copies, waits for them, and re-layouts  6.39 us (1%)
    pallas_call x3, Pallas kernels, pack(): pl.pallas_call(functools.partial(pack_kernel, tiles=tiles, slots=slots, s...  197 us
    all_to_all x4, blocking collectives, exchange(): return lax.all_to_all(source, 'cp', split_axis=0, concat_axis=0, tiled=True)  165 us
    pallas_call x4, Pallas kernels, attend(): pl.pallas_call(functools.partial(attend_kernel, tiles=tiles, docs=lengths...  43.1 us
    all_gather x2, waiting for transfers between devices, share(): lax.all_gather(own.reshape(tok_rows, kv_width), 'grp', axis=0, tiled=True)  14.2 us
    all_to_all x2, waiting for transfers between devices, exchange(): return lax.all_to_all(source, 'cp', split_axis=0, concat_axis=0, tiled=True)  11.6 us
  transfers between devices with their start and end apart: 4, of which 2 were waited for; matrix products, arithmetic and copies ran while one was open for 0% of the time, Pallas kernels for 15%

profile of v1, /device:TPU:0, one launch (start us, length us, event | category | flops | bytes accessed | tf_op | source)
XLA Modules:
  0.0 459.6 jit_solution(17352200282727541989)
XLA Ops:
  6.5 161.4 %shard_map.64 = (bf16[16,32,1024]{2,1,0:T(8,128)(2,1)}, bf16[16,32,1024]{2,1,0:T(8,128)(2,1)}, bf16[16,32,2048]{2,1,0:T(8,128)(2,1)}, bf16[16,32,2048]{2,1,0:T(8...) custom-call(s32[16]{0:T(128)} %bitcast.24, bf16[8,32,8192]{2,1,0:T(8,128)(2,1)} %bitcast.19, ...), custom_call_target="tpu_custom_call" | custom-call | tf_op jit(solution)/shard_map/pallas_call | solution.py:45
  168.0 0.0 copy-start.10
  168.0 0.0 copy-start.9
  168.0 33.5 %all_to_all.30.refs_0_ = bf16[16,32,1024]{2,1,0:T(8,128)(2,1)} all-to-all(bf16[16,32,1024]{2,1,0:T(8,128)(2,1)} %get-tuple-element.12), channel_id=1, replica_groups=mesh['cp'=8,'grp'=4] {'cp'}, dimensions={0} | all-to-all | bytes 2097152 | tf_op jit(solution)/shard_map/all_to_all | solution.py:137
  201.5 0.0 copy-done.10
  201.5 28.9 %all_to_all.31.refs_0_ = bf16[16,32,1024]{2,1,0:T(8,128)(2,1)} all-to-all(bf16[16,32,1024]{2,1,0:T(8,128)(2,1)S(1)} %copy-done.10), channel_id=1, replica_groups=mesh['cp'=8,'grp'=4] {'cp'}, dimensions={0} | all-to-all | bytes 2097152 | tf_op jit(solution)/shard_map/all_to_all | solution.py:137
  230.5 0.0 copy-done.9
  230.5 0.0 copy-start.8
  230.5 51.3 %all_to_all.32.refs_0_.refs_1_.refs_2_.refs_3_.refs_4_.refs_5_.refs_6_.refs_7_ = bf16[16,32,2048]{2,1,0:T(8,128)(2,1)S(1)} all-to-all(bf16[16,32,2048]{2,1,0:T(8,128)(2,1)S(1)} %copy-done.9), channel_id=1, replica_groups=mesh['cp'=8,'grp'=4] {'cp'}, dimensions={0} | all-to-all | bytes 4194304 | tf_op jit(solution)/shard_map/all_to_all | solution.py:137
  281.8 0.0 copy-done.8
  281.8 51.2 %all_to_all.33.refs_0_.refs_1_.refs_2_.refs_3_.refs_4_.refs_5_.refs_6_.refs_7_ = bf16[16,32,2048]{2,1,0:T(8,128)(2,1)} all-to-all(bf16[16,32,2048]{2,1,0:T(8,128)(2,1)S(1)} %copy-done.8), channel_id=1, replica_groups=mesh['cp'=8,'grp'=4] {'cp'}, dimensions={0} | all-to-all | bytes 4194304 | tf_op jit(solution)/shard_map/all_to_all | solution.py:137
  333.0 4.4 all-to-all-start.5
  337.4 0.0 all-gather.3.cloned.1.call-start
  337.4 17.7 %shard_map.65 = bf16[8,32,1024]{2,1,0:T(8,128)(2,1)} custom-call(s32[8]{0:T(128)} %bitcast.9, bf16[16,32,1024]{2,1,0:T(8,128)(2,1)} %all_to_all.30.refs_0_), custom_call_target="tpu_custom_call" | custom-call | tf_op jit(solution)/shard_map/pallas_call | solution.py:45
  355.2 0.0 all-gather.3.cloned.1.call-update
  355.2 0.0 all-gather.5.cloned.1.call-start
  355.2 17.7 %shard_map.66 = bf16[8,32,1024]{2,1,0:T(8,128)(2,1)} custom-call(s32[8]{0:T(128)} %bitcast.10, bf16[16,32,1024]{2,1,0:T(8,128)(2,1)} %all_to_all.31.refs_0_), custom_call_target="tpu_custom_call" | custom-call | tf_op jit(solution)/shard_map/pallas_call | solution.py:45
  373.0 0.0 all-gather.5.cloned.1.call-update
  373.0 11.6 %all-to-all-done.5.refs_0_.refs_1_.refs_2_.refs_3_.refs_4_.refs_5_.refs_6_.refs_7_ = bf16[16,32,2048]{2,1,0:T(8,128)(2,1)} async-done(((bf16[16,32,2048]{2,1,0:T(8,128)(2,1)}), bf16[16,32,2048]{2,1,0:T(8,128)(2,1)}, u32[]{:S(2)}, u32[]{:S(2)}) %all-to-all-start.5) | async-done | bytes 2097184 | tf_op jit(solution)/shard_map/all_to_all | solution.py:137
  384.6 0.0 copy-start.6
  384.6 0.0 copy-start.7
  384.6 4.5 all-to-all-start
  389.1 0.0 all-gather.3.cloned.1.call-done.refs_8_
  389.1 14.2 %all-gather.5.cloned.1.call-done.refs_9_ = bf16[1024,1024]{1,0:T(8,128)(2,1)} async-done(((bf16[256,1024]{1,0:T(8,128)(2,1)}), bf16[1024,1024]{1,0:T(8,128)(2,1)}) %all-gather.5.cloned.1.call-update) | async-done | bytes 2097168 | tf_op jit(solution)/shard_map/all_gather | solution.py:142
  403.3 0.0 copy-done.6
  403.3 0.0 copy-done.7
  403.3 0.0 copy-start.1
  403.3 1.6 copy-done.1
  404.9 0.0 copy-start.4
  404.9 1.6 copy-done.4
  406.5 0.0 copy-start
  406.5 0.0 copy-start.2
  406.5 11.5 %shard_map.67.refs_10_ = bf16[256,8192]{1,0:T(8,128)(2,1)} custom-call(s32[8]{0:T(128)S(1)} %bitcast.11, s32[3]{0:T(128)S(1)} %bitcast.15, s32[1]{0:T(128)} %bitcast.2.info_ref, bf16[16,32,2048]{2,1,0:T(8,128)(2,1)} %all-to-all-done.5.refs_0_.refs_1_.refs_2_.refs_3_.refs_4_.refs_5_.refs_6_.refs_7_, ...), custom_call_target="tpu_custom_call" | custom-call | flops 2147483648 | bytes 2097152 | tf_op jit(solution)/shard_map/pallas_call | solution.py:107
  418.0 0.0 copy-done
  418.0 0.0 copy-done.2
  418.0 10.3 %shard_map.68.refs_10_ = bf16[256,8192]{1,0:T(8,128)(2,1)} custom-call(s32[8]{0:T(128)S(1)} %bitcast.12, s32[3]{0:T(128)S(1)} %bitcast.16, s32[1]{0:T(128)} %bitcast.2.info_ref, bf16[16,32,2048]{2,1,0:T(8,128)(2,1)S(1)} %copy-done, bf16[16,32,2048]{2,1,0:T(8,128)(2,1)S(1)} %copy-done, ...), custom_call_target="tpu_custom_call", output_to_operand_aliasing={{}: (13, {})} | custom-call | flops 2147483648 | bytes 2097152 | tf_op jit(solution)/shard_map/pallas_call | solution.py:107
  428.3 10.4 %shard_map.69.refs_10_ = bf16[256,8192]{1,0:T(8,128)(2,1)} custom-call(s32[8]{0:T(128)S(1)} %bitcast.13, s32[3]{0:T(128)S(1)} %bitcast.17, s32[1]{0:T(128)} %bitcast.2.info_ref, bf16[16,32,2048]{2,1,0:T(8,128)(2,1)S(1)} %all_to_all.32.refs_0_.refs_1_.refs_2_.refs_3_.refs_4_.refs_5_.refs_6_.refs_7_, ...), custom_call_target="tpu_custom_call", output_to_operand_aliasing={{}: (13, {})} | custom-call | flops 2147483648 | bytes 2097152 | tf_op jit(solution)/shard_map/pallas_call | solution.py:107
  438.7 0.0 all-to-all-done.refs_0_.refs_1_.refs_2_.refs_3_.refs_4_.refs_5_.refs_6_.refs_7_
  438.7 0.0 copy-start.3
  438.7 1.6 copy-done.3
  440.3 0.0 copy-start.5
  440.3 1.6 copy-done.5
  441.9 10.9 %shard_map.70 = bf16[256,8192]{1,0:T(8,128)(2,1)} custom-call(s32[8]{0:T(128)S(1)} %bitcast.14, s32[3]{0:T(128)S(1)} %bitcast.18, s32[1]{0:T(128)} %bitcast.2.info_ref, bf16[16,32,2048]{2,1,0:T(8,128)(2,1)} %all-to-all-done.refs_0_.refs_1_.refs_2_.refs_3_.refs_4_.refs_5_.refs_6_.refs_7_, ...), custom_call_target="tpu_custom_call", output_to_operand_aliasing={{}: (13, {})} | custom-call | flops 2147483648 | bytes 2097152 | tf_op jit(solution)/shard_map/pallas_call | solution.py:107
Async XLA Ops:
  168.0 33.5 %copy-start.10 = (bf16[16,32,1024]{2,1,0:T(8,128)(2,1)S(1)}, bf16[16,32,1024]{2,1,0:T(8,128)(2,1)}, u32[]{:S(2)}) copy-start(bf16[16,32,1024]{2,1,0:T(8,128)(2,1)} %get-tuple-element.13) | copy-start | bytes 3145732
  168.0 62.5 %copy-start.9 = (bf16[16,32,2048]{2,1,0:T(8,128)(2,1)S(1)}, bf16[16,32,2048]{2,1,0:T(8,128)(2,1)}, u32[]{:S(2)}) copy-start(bf16[16,32,2048]{2,1,0:T(8,128)(2,1)} %get-tuple-element.14) | copy-start | bytes 6291460
  230.5 51.3 %copy-start.8 = (bf16[16,32,2048]{2,1,0:T(8,128)(2,1)S(1)}, bf16[16,32,2048]{2,1,0:T(8,128)(2,1)}, u32[]{:S(2)}) copy-start(bf16[16,32,2048]{2,1,0:T(8,128)(2,1)} %get-tuple-element.15) | copy-start | bytes 6291460
  333.0 51.6 %all-to-all-start.5 = ((bf16[16,32,2048]{2,1,0:T(8,128)(2,1)}), bf16[16,32,2048]{2,1,0:T(8,128)(2,1)}, u32[]{:S(2)}, u32[]{:S(2)}) async-start(bf16[16,32,2048]{2,1,0:T(8,128)(2,1)} %get-tuple-element.16), calls=%async_computation.5 | async-start | bytes 4194304 | tf_op jit(solution)/shard_map/all_to_all | solution.py:137
  337.4 51.8 %all-gather.3.cloned.1.call-start = ((), (), s32[]{:S(2)}) async-start(), calls=%async_computation.6 | async-start | bytes 2621440 | tf_op jit(solution)/shard_map/all_gather | solution.py:142
  355.2 48.1 %all-gather.5.cloned.1.call-start = ((), (), s32[]{:S(2)}) async-start(), calls=%async_computation.7 | async-start | bytes 2621440 | tf_op jit(solution)/shard_map/all_gather | solution.py:142
  384.6 18.7 %copy-start.6 = (s32[1,8]{1,0:T(1,128)S(1)}, s32[1,8]{1,0:T(1,128)}, u32[]{:S(2)}) copy-start(s32[1,8]{1,0:T(1,128)} %param.11) | copy-start | bytes 100
  384.6 18.7 %copy-start.7 = (s32[1,3]{1,0:T(1,128)S(1)}, s32[1,3]{1,0:T(1,128)}, u32[]{:S(2)}) copy-start(s32[1,3]{1,0:T(1,128)} %param.9) | copy-start | bytes 40
  384.6 54.1 %all-to-all-start = ((bf16[16,32,2048]{2,1,0:T(8,128)(2,1)}), bf16[16,32,2048]{2,1,0:T(8,128)(2,1)}, u32[]{:S(2)}, u32[]{:S(2)}) async-start(bf16[16,32,2048]{2,1,0:T(8,128)(2,1)} %get-tuple-element.11), calls=%async_computation | async-start | bytes 4194304 | tf_op jit(solution)/shard_map/all_to_all | solution.py:137
  403.3 1.6 copy-start.1
  404.9 1.6 copy-start.4
  406.5 11.5 %copy-start = (bf16[16,32,2048]{2,1,0:T(8,128)(2,1)S(1)}, bf16[16,32,2048]{2,1,0:T(8,128)(2,1)}, u32[]{:S(2)}) copy-start(bf16[16,32,2048]{2,1,0:T(8,128)(2,1)} %all_to_all.33.refs_0_.refs_1_.refs_2_.refs_3_.refs_4_.refs_5_.refs_6_.refs_7_) | copy-start | bytes 6291460
  406.5 11.5 %copy-start.2 = (bf16[1024,1024]{1,0:T(8,128)(2,1)S(1)}, bf16[1024,1024]{1,0:T(8,128)(2,1)}, u32[]{:S(2)}) copy-start(bf16[1024,1024]{1,0:T(8,128)(2,1)} %all-gather.3.cloned.1.call-done.refs_8_) | copy-start | bytes 6291460
  438.7 1.6 copy-start.3
  440.3 1.6 copy-start.5
Sparse Core Ops, SparseCore 0:
  355.3 23.7 all-gather.2
  380.7 22.5 all-gather.4

commit v2 on v1

--- a/solution.py
+++ b/solution.py
@@ -13,12 +13,13 @@
 HEAD_SIZE = 128
 PER_GROUP = QUERY_HEADS // KEY_VALUE_HEADS
 HEAD_WIDTH = PER_GROUP * HEAD_SIZE
-CHUNKS = 4
+PARTS = (6, 2)
 
 
-def pack_kernel(chosen_ref, *refs, tiles, slots, spans):
-    count = len(spans)
-    sources, targets, sems = refs[: len(refs) - 1 - count], refs[-1 - count : -1], refs[-1]
+def pack_kernel(chosen_ref, *refs, tiles, slots, count):
+    sources, target, sems = refs[:count], refs[count], refs[count + 1]
+    step = pl.program_id(0)
+    width = sources[0].shape[2]
 
     def each(act):
         def one(slot, carry):
@@ -26,9 +27,10 @@
 
             @pl.when(tile < tiles)
             def _():
-                for number, (source, start, width) in enumerate(spans):
-                    piece = sources[source].at[tile, :, pl.ds(start, width)]
-                    act(pltpu.make_async_copy(piece, targets[number].at[slot], sems.at[number, slot]))
+                for i, source in enumerate(sources):
+                    start = pl.multiple_of((step * count + i) * width, width)
+                    place = target.at[slot, :, pl.ds(start, width)]
+                    act(pltpu.make_async_copy(source.at[tile], place, sems.at[i, slot]))
 
             return carry
 
@@ -38,19 +40,23 @@
     each(lambda copy: copy.wait())
 
 
-def pack(chosen, arrays, spans, tile_rows):
-    tiles, slots = arrays[0].shape[0] // tile_rows, chosen.shape[0]
-    tiled = [a.reshape(tiles, tile_rows, a.shape[1]) for a in arrays]
-    any_spec = pl.BlockSpec(memory_space=pl.ANY)
+def pack(chosen, sources, tile_rows, width, first, steps):
+    tiles, slots, count = sources[0].shape[0] // tile_rows, chosen.shape[0], len(sources)
+    tiled = [a.reshape(tiles, tile_rows, a.shape[1]) for a in sources]
+    out_width = steps * count * width
     return pl.pallas_call(
-        functools.partial(pack_kernel, tiles=tiles, slots=slots, spans=spans),
-        out_shape=[jax.ShapeDtypeStruct((slots, tile_rows, w), jnp.bfloat16) for _, _, w in spans],
+        functools.partial(pack_kernel, tiles=tiles, slots=slots, count=count),
+        out_shape=jax.ShapeDtypeStruct((slots, tile_rows, out_width), jnp.bfloat16),
         grid_spec=pltpu.PrefetchScalarGridSpec(
             num_scalar_prefetch=1,
-            grid=(1,),
-            in_specs=[any_spec] * len(tiled),
-            out_specs=[any_spec] * len(spans),
-            scratch_shapes=[pltpu.SemaphoreType.DMA((len(spans), slots))],
+            grid=(steps,),
+            in_specs=[pl.BlockSpec((tiles, tile_rows, width), lambda j, c: (0, 0, first + j))] * count,
+            out_specs=pl.BlockSpec(memory_space=pl.ANY),
+            scratch_shapes=[pltpu.SemaphoreType.DMA((count, slots))],
+        ),
+        compiler_params=pltpu.CompilerParams(vmem_limit_bytes=40 * 2**20),
+        cost_estimate=pl.CostEstimate(
+            flops=0, bytes_accessed=4 * tiles * tile_rows * out_width, transcendentals=0
         ),
     )(chosen, *tiled)
 
@@ -88,16 +94,19 @@
         out_ref[:, span] = (summed / totals).astype(jnp.bfloat16)
 
 
-def attend(take, lengths, info, got, keys, values, result, first):
+def attend(take, lengths, info, got, shared, result, first):
     tiles, (_, tile_rows, width) = take.shape[0], got.shape
-    rows, length = tiles * tile_rows, keys.shape[0]
+    rows, length = tiles * tile_rows, shared.shape[0]
     heads = width // HEAD_WIDTH
     in_specs = [
         pl.BlockSpec((1, tile_rows, HEAD_WIDTH), lambda h, t, e, n, i=i: (t[i], 0, h))
         for i in range(tiles)
     ]
-    in_specs += [pl.BlockSpec((length, HEAD_SIZE), lambda h, t, e, n: (0, first + h))] * 2
-    operands = [got] * tiles + [keys, values]
+    in_specs += [
+        pl.BlockSpec((length, HEAD_SIZE), lambda h, t, e, n, b=b: (0, b + first + h))
+        for b in (0, KEY_VALUE_HEADS)
+    ]
+    operands = [got] * tiles + [shared, shared]
     aliases = {}
     if result is not None:
         in_specs.append(pl.BlockSpec(memory_space=pl.ANY))
@@ -128,27 +137,23 @@
     tile_rows = tok_rows // peer_count
     chosen, placed = send_tile[0], take_slot[0]
     kv_width = KEY_VALUE_HEADS * HEAD_SIZE
-    q_width = QUERY_HEADS * HEAD_SIZE // CHUNKS
-    spans = [(1, 0, kv_width), (2, 0, kv_width)]
-    spans += [(0, i * q_width, q_width) for i in range(CHUNKS)]
-    sent = pack(chosen, [queries, keys, values], spans, tile_rows)
 
     def exchange(source):
         return lax.all_to_all(source, "cp", split_axis=0, concat_axis=0, tiled=True)
 
-    def share(source):
-        got = exchange(source).reshape(-1, kv_width)
-        (own,) = pack(placed, [got], [(0, 0, kv_width)], tile_rows)
-        return lax.all_gather(own.reshape(tok_rows, kv_width), "grp", axis=0, tiled=True)
-
-    all_keys, all_values = share(sent[0]), share(sent[1])
-    lengths = doc_lengths[0]
     info = (lax.axis_index("grp") * tok_rows).astype(jnp.int32).reshape(1)
-    result = None
-    for i in range(CHUNKS):
-        got = exchange(sent[2 + i])
-        first = i * (KEY_VALUE_HEADS // CHUNKS)
-        result = attend(placed, lengths, info, got, all_keys, all_values, result, first)
+    got = exchange(pack(chosen, [keys, values], tile_rows, kv_width, 0, 1))
+    owned, shared = got.reshape(-1, 2 * kv_width), None
+    result, first = None, 0
+    for heads in PARTS:
+        packed = pack(chosen, [queries], tile_rows, HEAD_WIDTH, first, heads)
+        packed, got = lax.optimization_barrier((packed, got))
+        got = exchange(packed)
+        if shared is None:
+            owned = pack(placed, [owned], tile_rows, 2 * kv_width, 0, 1)
+            shared = lax.all_gather(owned.reshape(tok_rows, 2 * kv_width), "grp", axis=0, tiled=True)
+        result = attend(placed, doc_lengths[0], info, got, shared, result, first)
+        first += heads
     return result
 
 

time: 460 us -> 282 us (0.61)
  Pallas kernels: 240 us -> 47.7 us
  blocking collectives: 165 us -> 0 us
  waiting for transfers between devices: 25.8 us -> 187 us
  local copies, waits for them, and re-layouts: 6.39 us -> 16.7 us
  starting transfers between devices: 8.96 us -> 15.7 us
    pallas_call x3 -> x4, Pallas kernels: 197 us -> 9.15 us  [pack(): pl.pallas_call(functools.partial(pack_kernel, tiles=tiles, slots=slots, c...]
    all_to_all x2 -> x3, waiting for transfers between devices: 11.6 us -> 187 us  [exchange(): return lax.all_to_all(source, 'cp', split_axis=0, concat_axis=0, tiled=True)]
    all_to_all x4 -> x0, blocking collectives: 165 us -> none  [exchange(): return lax.all_to_all(source, 'cp', split_axis=0, concat_axis=0, tiled=True)]
    all_gather x2 -> x1, waiting for transfers between devices: 14.2 us -> 0.01 us  [local(): lax.all_gather(owned.reshape(tok_rows, 2 * kv_width), 'grp', axis=0, tile...]
    unnamed x22 -> x26, local copies, waits for them, and re-layouts: 6.39 us -> 16.7 us
    all_to_all x2 -> x3, starting transfers between devices: 8.87 us -> 15.6 us  [exchange(): return lax.all_to_all(source, 'cp', split_axis=0, concat_axis=0, tiled=True)]
    pallas_call x4 -> x2, Pallas kernels: 43.1 us -> 38.5 us  [attend(): pl.pallas_call(functools.partial(attend_kernel, tiles=tiles, docs=lengths...]
  transfers between devices with their start and end apart: 4 -> 4, of which waited for: 2 -> 3; matrix products, arithmetic and copies ran while one was open for 0% -> 0% of each run, Pallas kernels for 15% -> 13%
where the time goes in v2:
time: 282 us; the launch traced here: 281 us
  waiting for transfers between devices  187 us (66%)
  Pallas kernels  47.7 us (17%)
  local copies, waits for them, and re-layouts  16.7 us (6%)
  starting transfers between devices  15.7 us (6%)
  between operations  13.5 us (5%)
    all_to_all x3, waiting for transfers between devices, exchange(): return lax.all_to_all(source, 'cp', split_axis=0, concat_axis=0, tiled=True)  187 us
    pallas_call x2, Pallas kernels, attend(): pl.pallas_call(functools.partial(attend_kernel, tiles=tiles, docs=lengths...  38.5 us
    unnamed x26, local copies, waits for them, and re-layouts  16.7 us
    all_to_all x3, starting transfers between devices, exchange(): return lax.all_to_all(source, 'cp', split_axis=0, concat_axis=0, tiled=True)  15.6 us
    pallas_call x4, Pallas kernels, pack(): pl.pallas_call(functools.partial(pack_kernel, tiles=tiles, slots=slots, c...  9.15 us
  transfers between devices with their start and end apart: 4, of which 3 were waited for; matrix products, arithmetic and copies ran while one was open for 0% of the time, Pallas kernels for 13%

profile of v2, /device:TPU:0, one launch (start us, length us, event | category | flops | bytes accessed | tf_op | source)
XLA Modules:
  0.0 281.0 jit_solution(3714904442479129220)
XLA Ops:
  6.5 0.0 copy-start.10
  6.5 0.0 copy-start.7
  6.5 1.1 copy-done.7
  7.6 0.0 copy-start.8
  7.6 1.0 copy-done.8
  8.6 0.0 copy-start.9
  8.6 0.7 copy-done.9
  9.3 1.5 shard_map.66
  10.8 0.0 copy-start.6
  10.9 1.3 copy-done.6
  12.2 7.3 %all-to-all-start = ((bf16[16,32,2048]{2,1,0:T(8,128)(2,1)}), bf16[16,32,2048]{2,1,0:T(8,128)(2,1)S(1)}, u32[]{:S(2)}, u32[]{:S(2)}) async-start(bf16[16,32,2048]{2,1,0:T(8,128)(2,1)} %copy-done.6), calls=%async_computation | async-start | bytes 4194304 | tf_op jit(solution)/shard_map/all_to_all | solution.py:142
  19.4 0.0 copy-done.10
  19.4 0.0 copy-start.3
  19.4 2.2 copy-done.3
  21.6 4.2 %shard_map.65 = bf16[16,32,6144]{2,1,0:T(8,128)(2,1)S(1)} custom-call(s32[16]{0:T(128)S(1)} %bitcast.13, bf16[8,32,8192]{2,1,0:T(8,128)(2,1)S(1)} %bitcast.8), custom_call_target="tpu_custom_call" | custom-call | bytes 6291456 | tf_op jit(solution)/shard_map/pallas_call | solution.py:47
  25.8 0.0 copy-start.2
  25.8 2.6 copy-done.2
  28.4 0.0 copy-start.11
  28.4 39.2 %all-to-all-done.refs_0_ = bf16[16,32,2048]{2,1,0:T(8,128)(2,1)S(1)} async-done(((bf16[16,32,2048]{2,1,0:T(8,128)(2,1)}), bf16[16,32,2048]{2,1,0:T(8,128)(2,1)S(1)}, u32[]{:S(2)}, u32[]{:S(2)}) %all-to-all-start) | async-done | bytes 2097184 | tf_op jit(solution)/shard_map/all_to_all | solution.py:142
  67.7 4.7 %all-to-all-start.1 = ((bf16[16,32,6144]{2,1,0:T(8,128)(2,1)}), bf16[16,32,6144]{2,1,0:T(8,128)(2,1)}, u32[]{:S(2)}, u32[]{:S(2)}) async-start(bf16[16,32,6144]{2,1,0:T(8,128)(2,1)} %copy-done.2), calls=%async_computation.1 | async-start | bytes 12582912 | tf_op jit(solution)/shard_map/all_to_all | solution.py:142
  72.4 0.0 all-gather.2.cloned.1.call-start
  72.4 0.0 copy-done.11
  72.5 1.6 shard_map.67
  74.0 0.0 all-gather.2.cloned.1.call-update
  74.1 0.0 copy-start.4
  74.1 2.2 copy-done.4
  76.3 0.0 copy-start.12
  76.3 1.9 shard_map.64
  78.1 0.0 copy-start.5
  78.1 1.3 copy-done.5
  79.5 130.2 %all-to-all-done.1.refs_0_.refs_1_.refs_2_.refs_3_.refs_4_.refs_5_.refs_6_.refs_7_ = bf16[16,32,6144]{2,1,0:T(8,128)(2,1)} async-done(((bf16[16,32,6144]{2,1,0:T(8,128)(2,1)}), bf16[16,32,6144]{2,1,0:T(8,128)(2,1)}, u32[]{:S(2)}, u32[]{:S(2)}) %all-to-all-start.1) | async-done | bytes 6291488 | tf_op jit(solution)/shard_map/all_to_all | solution.py:142
  209.7 3.6 %all-to-all-start.2 = ((bf16[16,32,2048]{2,1,0:T(8,128)(2,1)}), bf16[16,32,2048]{2,1,0:T(8,128)(2,1)S(1)}, u32[]{:S(2)}, u32[]{:S(2)}) async-start(bf16[16,32,2048]{2,1,0:T(8,128)(2,1)} %copy-done.5), calls=%async_computation.2 | async-start | bytes 4194304 | tf_op jit(solution)/shard_map/all_to_all | solution.py:142
  213.3 0.0 all-gather.2.cloned.1.call-done.refs_8_.refs_9_
  213.4 0.0 copy-done.12
  213.4 0.0 copy-start
  213.4 2.2 copy-done
  215.6 28.3 %shard_map.68.refs_10_ = bf16[256,8192]{1,0:T(8,128)(2,1)} custom-call(s32[8]{0:T(128)S(1)} %bitcast.16, s32[3]{0:T(128)S(1)} %bitcast.18, s32[1]{0:T(128)} %bitcast.2.info_ref, bf16[16,32,6144]{2,1,0:T(8,128)(2,1)} %all-to-all-done.1.refs_0_.refs_1_.refs_2_.refs_3_.refs_4_.refs_5_.refs_6_.refs_7_, ...), custom_call_target="tpu_custom_call" | custom-call | flops 6442450944 | bytes 6291456 | tf_op jit(solution)/shard_map/pallas_call | solution.py:116
  243.8 17.9 %all-to-all-done.2.refs_0_.refs_1_.refs_2_.refs_3_.refs_4_.refs_5_.refs_6_.refs_7_ = bf16[16,32,2048]{2,1,0:T(8,128)(2,1)S(1)} async-done(((bf16[16,32,2048]{2,1,0:T(8,128)(2,1)}), bf16[16,32,2048]{2,1,0:T(8,128)(2,1)S(1)}, u32[]{:S(2)}, u32[]{:S(2)}) %all-to-all-start.2) | async-done | bytes 2097184 | tf_op jit(solution)/shard_map/all_to_all | solution.py:142
  261.7 0.0 copy-start.1
  261.7 2.2 copy-done.1
  263.9 10.3 %shard_map.69 = bf16[256,8192]{1,0:T(8,128)(2,1)} custom-call(s32[8]{0:T(128)S(1)} %bitcast.17, s32[3]{0:T(128)S(1)} %bitcast.19, s32[1]{0:T(128)} %bitcast.2.info_ref, bf16[16,32,2048]{2,1,0:T(8,128)(2,1)S(1)} %all-to-all-done.2.refs_0_.refs_1_.refs_2_.refs_3_.refs_4_.refs_5_.refs_6_.refs_7_, ...), custom_call_target="tpu_custom_call", output_to_operand_aliasing={{}: (13, {})} | custom-call | flops 2147483648 | bytes 2097152 | tf_op jit(solution)/shard_map/pallas_call | solution.py:116
Async XLA Ops:
  6.5 12.9 %copy-start.10 = (s32[1,16]{1,0:T(1,128)S(1)}, s32[1,16]{1,0:T(1,128)}, u32[]{:S(2)}) copy-start(s32[1,16]{1,0:T(1,128)} %param.10) | copy-start | bytes 196
  6.5 1.1 copy-start.7
  7.6 1.0 copy-start.8
  8.6 0.7 copy-start.9
  10.8 1.3 copy-start.6
  12.2 55.5 %all-to-all-start = ((bf16[16,32,2048]{2,1,0:T(8,128)(2,1)}), bf16[16,32,2048]{2,1,0:T(8,128)(2,1)S(1)}, u32[]{:S(2)}, u32[]{:S(2)}) async-start(bf16[16,32,2048]{2,1,0:T(8,128)(2,1)} %copy-done.6), calls=%async_computation | async-start | bytes 4194304 | tf_op jit(solution)/shard_map/all_to_all | solution.py:142
  19.4 2.2 copy-start.3
  25.8 2.6 copy-start.2
  28.4 44.0 %copy-start.11 = (s32[1,8]{1,0:T(1,128)S(1)}, s32[1,8]{1,0:T(1,128)}, u32[]{:S(2)}) copy-start(s32[1,8]{1,0:T(1,128)} %param.11) | copy-start | bytes 100
  67.7 142.0 %all-to-all-start.1 = ((bf16[16,32,6144]{2,1,0:T(8,128)(2,1)}), bf16[16,32,6144]{2,1,0:T(8,128)(2,1)}, u32[]{:S(2)}, u32[]{:S(2)}) async-start(bf16[16,32,6144]{2,1,0:T(8,128)(2,1)} %copy-done.2), calls=%async_computation.1 | async-start | bytes 12582912 | tf_op jit(solution)/shard_map/all_to_all | solution.py:142
  72.4 140.9 %all-gather.2.cloned.1.call-start = ((), (), s32[]{:S(2)}) async-start(), calls=%async_computation.3 | async-start | bytes 5242880 | tf_op jit(solution)/shard_map/all_gather | solution.py:154
  74.1 2.2 copy-start.4
  76.3 137.1 %copy-start.12 = (s32[1,3]{1,0:T(1,128)S(1)}, s32[1,3]{1,0:T(1,128)}, u32[]{:S(2)}) copy-start(s32[1,3]{1,0:T(1,128)} %param.9) | copy-start | bytes 40
  78.1 1.3 copy-start.5
  209.7 52.0 %all-to-all-start.2 = ((bf16[16,32,2048]{2,1,0:T(8,128)(2,1)}), bf16[16,32,2048]{2,1,0:T(8,128)(2,1)S(1)}, u32[]{:S(2)}, u32[]{:S(2)}) async-start(bf16[16,32,2048]{2,1,0:T(8,128)(2,1)} %copy-done.5), calls=%async_computation.2 | async-start | bytes 4194304 | tf_op jit(solution)/shard_map/all_to_all | solution.py:142
  213.4 2.2 copy-start
  261.7 2.2 copy-start.1
Sparse Core Ops, SparseCore 0:
  74.8 35.8 all-gather.1

commit v3 on v2

--- a/solution.py
+++ b/solution.py
@@ -18,7 +18,6 @@
 
 def pack_kernel(chosen_ref, *refs, tiles, slots, count):
     sources, target, sems = refs[:count], refs[count], refs[count + 1]
-    step = pl.program_id(0)
     width = sources[0].shape[2]
 
     def each(act):
@@ -28,8 +27,7 @@
             @pl.when(tile < tiles)
             def _():
                 for i, source in enumerate(sources):
-                    start = pl.multiple_of((step * count + i) * width, width)
-                    place = target.at[slot, :, pl.ds(start, width)]
+                    place = target.at[slot, :, pl.ds(i * width, width)]
                     act(pltpu.make_async_copy(source.at[tile], place, sems.at[i, slot]))
 
             return carry
@@ -40,17 +38,19 @@
     each(lambda copy: copy.wait())
 
 
-def pack(chosen, sources, tile_rows, width, first, steps):
+def pack(chosen, sources, blocks, tile_rows, width):
     tiles, slots, count = sources[0].shape[0] // tile_rows, chosen.shape[0], len(sources)
     tiled = [a.reshape(tiles, tile_rows, a.shape[1]) for a in sources]
-    out_width = steps * count * width
+    out_width = count * width
     return pl.pallas_call(
         functools.partial(pack_kernel, tiles=tiles, slots=slots, count=count),
         out_shape=jax.ShapeDtypeStruct((slots, tile_rows, out_width), jnp.bfloat16),
         grid_spec=pltpu.PrefetchScalarGridSpec(
             num_scalar_prefetch=1,
-            grid=(steps,),
-            in_specs=[pl.BlockSpec((tiles, tile_rows, width), lambda j, c: (0, 0, first + j))] * count,
+            grid=(1,),
+            in_specs=[
+                pl.BlockSpec((tiles, tile_rows, width), lambda j, c, b=b: (0, 0, b)) for b in blocks
+            ],
             out_specs=pl.BlockSpec(memory_space=pl.ANY),
             scratch_shapes=[pltpu.SemaphoreType.DMA((count, slots))],
         ),
@@ -94,12 +94,11 @@
         out_ref[:, span] = (summed / totals).astype(jnp.bfloat16)
 
 
-def attend(take, lengths, info, got, shared, result, first):
-    tiles, (_, tile_rows, width) = take.shape[0], got.shape
+def attend(take, lengths, info, got, shared, result, first, heads, skip):
+    tiles, tile_rows = take.shape[0], got.shape[1]
     rows, length = tiles * tile_rows, shared.shape[0]
-    heads = width // HEAD_WIDTH
     in_specs = [
-        pl.BlockSpec((1, tile_rows, HEAD_WIDTH), lambda h, t, e, n, i=i: (t[i], 0, h))
+        pl.BlockSpec((1, tile_rows, HEAD_WIDTH), lambda h, t, e, n, i=i: (t[i], 0, skip + h))
         for i in range(tiles)
     ]
     in_specs += [
@@ -126,7 +125,7 @@
         input_output_aliases=aliases,
         compiler_params=pltpu.CompilerParams(vmem_limit_bytes=40 * 2**20),
         cost_estimate=pl.CostEstimate(
-            flops=4 * pairs * HEAD_SIZE, bytes_accessed=2 * rows * width * 2, transcendentals=pairs
+            flops=4 * pairs * HEAD_SIZE, bytes_accessed=4 * rows * heads * HEAD_WIDTH, transcendentals=pairs
         ),
     )(take, lengths, info, *operands)
 
@@ -142,19 +141,19 @@
         return lax.all_to_all(source, "cp", split_axis=0, concat_axis=0, tiled=True)
 
     info = (lax.axis_index("grp") * tok_rows).astype(jnp.int32).reshape(1)
-    got = exchange(pack(chosen, [keys, values], tile_rows, kv_width, 0, 1))
-    owned, shared = got.reshape(-1, 2 * kv_width), None
-    result, first = None, 0
-    for heads in PARTS:
-        packed = pack(chosen, [queries], tile_rows, HEAD_WIDTH, first, heads)
-        packed, got = lax.optimization_barrier((packed, got))
-        got = exchange(packed)
-        if shared is None:
-            owned = pack(placed, [owned], tile_rows, 2 * kv_width, 0, 1)
-            shared = lax.all_gather(owned.reshape(tok_rows, 2 * kv_width), "grp", axis=0, tiled=True)
-        result = attend(placed, doc_lengths[0], info, got, shared, result, first)
-        first += heads
-    return result
+    early, late = PARTS
+    sources, blocks = [keys, values] + [queries] * early, [0, 0] + list(range(early))
+    got = exchange(pack(chosen, sources, blocks, tile_rows, HEAD_WIDTH))
+    sources, blocks = [queries] * late, list(range(early, early + late))
+    packed = pack(chosen, sources, blocks, tile_rows, HEAD_WIDTH)
+    packed, got = lax.optimization_barrier((packed, got))
+    rest = exchange(packed)
+    received = got.reshape(-1, got.shape[2])
+    owned = pack(placed, [received], [0], tile_rows, 2 * kv_width).reshape(tok_rows, 2 * kv_width)
+    shared = lax.all_gather(owned, "grp", axis=0, tiled=True)
+    lengths, skip = doc_lengths[0], 2 * kv_width // HEAD_WIDTH
+    result = attend(placed, lengths, info, got, shared, None, 0, early, skip)
+    return attend(placed, lengths, info, rest, shared, result, early, late, 0)
 
 
 def solution(mesh):

time: 282 us -> 296 us (1.050)
  waiting for transfers between devices: 187 us -> 208 us
  starting transfers between devices: 15.7 us -> 11.1 us
    all_gather x1, waiting for transfers between devices: 0.01 us -> 30.1 us  [local(): shared = lax.all_gather(owned, 'grp', axis=0, tiled=True)]
    all_to_all x3 -> x2, waiting for transfers between devices: 187 us -> 178 us  [exchange(): return lax.all_to_all(source, 'cp', split_axis=0, concat_axis=0, tiled=True)]
    all_to_all x3 -> x2, starting transfers between devices: 15.6 us -> 11 us  [exchange(): return lax.all_to_all(source, 'cp', split_axis=0, concat_axis=0, tiled=True)]
    unnamed x26 -> x24, local copies, waits for them, and re-layouts: 16.7 us -> 16.1 us
    pallas_call x4 -> x3, Pallas kernels: 9.15 us -> 8.5 us  [pack(): pl.pallas_call(functools.partial(pack_kernel, tiles=tiles, slots=slots, c...]
  transfers between devices with their start and end apart: 4 -> 3, of which waited for: 3 -> 2; matrix products, arithmetic and copies ran while one was open for 0% -> 0% of each run, Pallas kernels for 13% -> 10%
where the time goes in v3:
time: 296 us
  waiting for transfers between devices  208 us (70%)
  Pallas kernels  47.1 us (16%)
  local copies, waits for them, and re-layouts  16.1 us (5%)
  between operations  13.5 us (5%)
  starting transfers between devices  11.1 us (4%)
    all_to_all x2, waiting for transfers between devices, exchange(): return lax.all_to_all(source, 'cp', split_axis=0, concat_axis=0, tiled=True)  178 us
    pallas_call x2, Pallas kernels, attend(): pl.pallas_call(functools.partial(attend_kernel, tiles=tiles, docs=lengths...  38.6 us
    all_gather x1, waiting for transfers between devices, local(): shared = lax.all_gather(owned, 'grp', axis=0, tiled=True)  30.1 us
    unnamed x24, local copies, waits for them, and re-layouts  16.1 us
    all_to_all x2, starting transfers between devices, exchange(): return lax.all_to_all(source, 'cp', split_axis=0, concat_axis=0, tiled=True)  11 us
    pallas_call x3, Pallas kernels, pack(): pl.pallas_call(functools.partial(pack_kernel, tiles=tiles, slots=slots, c...  8.5 us
  transfers between devices with their start and end apart: 3, of which 2 were waited for; matrix products, arithmetic and copies ran while one was open for 0% of the time, Pallas kernels for 10%

profile of v3, /device:TPU:0, one launch (start us, length us, event | category | flops | bytes accessed | tf_op | source)
XLA Modules:
  0.0 295.8 jit_solution(5576232150910602369)
XLA Ops:
  6.5 0.0 copy-start
  6.5 2.2 copy-done
  8.7 0.0 copy-start.6
  8.7 1.0 copy-done.6
  9.8 0.0 copy-start.7
  9.8 1.0 copy-done.7
  10.8 0.0 copy-start.10
  10.8 0.7 copy-done.10
  11.5 3.7 %shard_map.65 = bf16[16,32,8192]{2,1,0:T(8,128)(2,1)S(1)} custom-call(s32[16]{0:T(128)S(1)} %bitcast.23, bf16[8,32,1024]{2,1,0:T(8,128)(2,1)S(1)} %bitcast.16, bf16[8,32,1024]{2,1,0:T(8,128)(2,1)S(1)} %bitcast.17, bf16[8,32,8192]{2,1,0:T(8,128)(2,1)S(1)} %bitcast.8, bf16[8,32,8192]{2,1,0:T(8,128)(2,1)S(1)} %bitcast.9, bf16[8,32,8192]{2,1,0:T(8,128)(2,1)S(1)} %bitcast.10, ...), custom_call_target="tpu_custom_call" | custom-call | bytes 8388608 | tf_op jit(solution)/shard_map/pallas_call | solution.py:45
  15.2 0.0 copy-start.4
  15.2 3.2 %copy-done.4 = bf16[16,32,8192]{2,1,0:T(8,128)(2,1)} copy-done((bf16[16,32,8192]{2,1,0:T(8,128)(2,1)}, bf16[16,32,8192]{2,1,0:T(8,128)(2,1)S(1)}, u32[]{:S(2)}) %copy-start.4) | copy-done | bytes 8388632
  18.5 0.0 copy-start.11
  18.5 7.4 %all-to-all-start = ((bf16[16,32,8192]{2,1,0:T(8,128)(2,1)}), bf16[16,32,8192]{2,1,0:T(8,128)(2,1)}, u32[]{:S(2)}, u32[]{:S(2)}) async-start(bf16[16,32,8192]{2,1,0:T(8,128)(2,1)} %copy-done.4), calls=%async_computation | async-start | bytes 16777216 | tf_op jit(solution)/shard_map/all_to_all | solution.py:141
  25.8 0.0 all-gather.2.cloned.1.call-start
  25.9 0.0 copy-done.11
  25.9 0.0 copy-start.1
  25.9 2.2 copy-done.1
  28.1 0.0 copy-start.8
  28.1 1.6 shard_map.64
  29.7 0.0 copy-start.5
  29.7 1.3 copy-done.5
  31.0 178.0 %all-to-all-done.refs_0_.refs_1_.refs_2_.refs_3_.refs_4_.refs_5_.refs_6_.refs_7_ = bf16[16,32,8192]{2,1,0:T(8,128)(2,1)} async-done(((bf16[16,32,8192]{2,1,0:T(8,128)(2,1)}), bf16[16,32,8192]{2,1,0:T(8,128)(2,1)}, u32[]{:S(2)}, u32[]{:S(2)}) %all-to-all-start) | async-done | bytes 8388640 | tf_op jit(solution)/shard_map/all_to_all | solution.py:141
  209.0 0.0 copy-done.8
  209.0 3.2 %shard_map.66 = bf16[8,32,2048]{2,1,0:T(8,128)(2,1)} custom-call(s32[8]{0:T(128)S(1)} %bitcast.18, bf16[16,32,8192]{2,1,0:T(8,128)(2,1)} %all-to-all-done.refs_0_.refs_1_.refs_2_.refs_3_.refs_4_.refs_5_.refs_6_.refs_7_), custom_call_target="tpu_custom_call" | custom-call | bytes 4194304 | tf_op jit(solution)/shard_map/pallas_call | solution.py:45
  212.2 0.0 copy-start.9
  212.2 0.0 all-gather.2.cloned.1.call-update
  212.2 3.6 %all-to-all-start.1 = ((bf16[16,32,2048]{2,1,0:T(8,128)(2,1)}), bf16[16,32,2048]{2,1,0:T(8,128)(2,1)S(1)}, u32[]{:S(2)}, u32[]{:S(2)}) async-start(bf16[16,32,2048]{2,1,0:T(8,128)(2,1)} %copy-done.5), calls=%async_computation.1 | async-start | bytes 4194304 | tf_op jit(solution)/shard_map/all_to_all | solution.py:141
  215.9 30.1 %all-gather.2.cloned.1.call-done.refs_8_.refs_9_ = bf16[1024,2048]{1,0:T(8,128)(2,1)} async-done(((bf16[256,2048]{1,0:T(8,128)(2,1)}), bf16[1024,2048]{1,0:T(8,128)(2,1)}) %all-gather.2.cloned.1.call-update) | async-done | bytes 4194320 | tf_op jit(solution)/shard_map/all_gather | solution.py:153
  245.9 0.0 copy-done.9
  245.9 0.0 copy-start.2
  245.9 2.2 copy-done.2
  248.1 28.3 %shard_map.67.refs_10_ = bf16[256,8192]{1,0:T(8,128)(2,1)} custom-call(s32[8]{0:T(128)S(1)} %bitcast.19, s32[3]{0:T(128)S(1)} %bitcast.21, s32[1]{0:T(128)} %bitcast.2.info_ref, bf16[16,32,8192]{2,1,0:T(8,128)(2,1)} %all-to-all-done.refs_0_.refs_1_.refs_2_.refs_3_.refs_4_.refs_5_.refs_6_.refs_7_, ...), custom_call_target="tpu_custom_call" | custom-call | flops 6442450944 | bytes 6291456 | tf_op jit(solution)/shard_map/pallas_call | solution.py:115
  276.4 0.0 all-to-all-done.1.refs_0_.refs_1_.refs_2_.refs_3_.refs_4_.refs_5_.refs_6_.refs_7_
  276.4 0.0 copy-start.3
  276.5 2.2 copy-done.3
  278.6 10.3 %shard_map.68 = bf16[256,8192]{1,0:T(8,128)(2,1)} custom-call(s32[8]{0:T(128)S(1)} %bitcast.20, s32[3]{0:T(128)S(1)} %bitcast.22, s32[1]{0:T(128)} %bitcast.2.info_ref, bf16[16,32,2048]{2,1,0:T(8,128)(2,1)S(1)} %all-to-all-done.1.refs_0_.refs_1_.refs_2_.refs_3_.refs_4_.refs_5_.refs_6_.refs_7_, ...), custom_call_target="tpu_custom_call", output_to_operand_aliasing={{}: (13, {})} | custom-call | flops 2147483648 | bytes 2097152 | tf_op jit(solution)/shard_map/pallas_call | solution.py:115
Async XLA Ops:
  6.5 2.2 copy-start
  8.7 1.0 copy-start.6
  9.8 1.0 copy-start.7
  10.8 0.7 copy-start.10
  15.2 3.2 %copy-start.4 = (bf16[16,32,8192]{2,1,0:T(8,128)(2,1)}, bf16[16,32,8192]{2,1,0:T(8,128)(2,1)S(1)}, u32[]{:S(2)}) copy-start(bf16[16,32,8192]{2,1,0:T(8,128)(2,1)S(1)} %shard_map.65) | copy-start | bytes 25165828
  18.5 7.4 %copy-start.11 = (s32[1,16]{1,0:T(1,128)S(1)}, s32[1,16]{1,0:T(1,128)}, u32[]{:S(2)}) copy-start(s32[1,16]{1,0:T(1,128)} %param.10) | copy-start | bytes 196
  18.5 190.6 %all-to-all-start = ((bf16[16,32,8192]{2,1,0:T(8,128)(2,1)}), bf16[16,32,8192]{2,1,0:T(8,128)(2,1)}, u32[]{:S(2)}, u32[]{:S(2)}) async-start(bf16[16,32,8192]{2,1,0:T(8,128)(2,1)} %copy-done.4), calls=%async_computation | async-start | bytes 16777216 | tf_op jit(solution)/shard_map/all_to_all | solution.py:141
  25.8 220.1 %all-gather.2.cloned.1.call-start = ((), (), s32[]{:S(2)}) async-start(), calls=%async_computation.2 | async-start | bytes 5242880 | tf_op jit(solution)/shard_map/all_gather | solution.py:153
  25.9 2.2 copy-start.1
  28.1 180.9 %copy-start.8 = (s32[1,8]{1,0:T(1,128)S(1)}, s32[1,8]{1,0:T(1,128)}, u32[]{:S(2)}) copy-start(s32[1,8]{1,0:T(1,128)} %param.11) | copy-start | bytes 100
  29.7 1.3 copy-start.5
  212.2 33.8 %copy-start.9 = (s32[1,3]{1,0:T(1,128)S(1)}, s32[1,3]{1,0:T(1,128)}, u32[]{:S(2)}) copy-start(s32[1,3]{1,0:T(1,128)} %param.9) | copy-start | bytes 40
  212.2 64.2 %all-to-all-start.1 = ((bf16[16,32,2048]{2,1,0:T(8,128)(2,1)}), bf16[16,32,2048]{2,1,0:T(8,128)(2,1)S(1)}, u32[]{:S(2)}, u32[]{:S(2)}) async-start(bf16[16,32,2048]{2,1,0:T(8,128)(2,1)} %copy-done.5), calls=%async_computation.1 | async-start | bytes 4194304 | tf_op jit(solution)/shard_map/all_to_all | solution.py:141
  245.9 2.2 copy-start.2
  276.4 2.2 copy-start.3
Sparse Core Ops, SparseCore 0:
  212.3 33.5 all-gather.1
